TPU v7x, 32 devices: a whole 2x2x4 slice. The times are simulated.
32 devices in a mesh: groups: 2 (over y), row: 2 (over core), col: 8 (over z, x).
Axes of the slice: x: 2, y: 2, z: 4, core: 2. Of those that a mesh axis runs over, the one named last changes fastest.
Arguments:
- block_values: float32 [160, 2, 64, 640], P(('groups', 'col'), 'row'), parts along dimension 0, may hold values from -1.2 to 1.2
- block_cols: int32 [160, 2, 10], P(('groups', 'col'), 'row'), parts along dimension 0, may hold values from -1 to 79, as said below
Outputs:
- block_product: float32 [160, 2, 64, 640], P(('groups', 'col'), 'row'), parts along dimension 0
There are 2 independent parts, one for each index of `groups`. A program takes and returns all parts, laid end to end along the dimension named above; each array names one. Nothing has to cross between parts.
Inputs may be any that keep to these rules, and one draw needn't show every extreme that they name: Each live entry of block_cols[i, p, :] is a block column j with j % 2 == p and |j - i| <= 10; the live entries of one list are distinct and stand before its -1 entries; every list holds at least one live entry; some list holds 10; how many are live varies from band to band.
All inputs are finite; a program needn't handle non-finite values.
Results may differ from a plain program's by a relative error of at most 0.0003.
Values sent between devices are 32-bit elements; how exact they have to be, the bound alone decides.
A program may use at most 128 MiB of HBM per device.

v0:
```python
import jax
import jax.numpy as jnp
from jax import lax
from jax.sharding import PartitionSpec as P

REACH = 10


def shifted(shard, axis, by):
    size = lax.axis_size(axis)
    pairs = [(i, i + by) for i in range(size) if 0 <= i + by < size]
    return lax.ppermute(shard, axis, pairs)


def shift_whole(payload, offset):
    return shifted((payload[0], payload[1]), "col", offset)


def local(block_values, block_cols):
    band_rows = block_values.shape[0]
    block_side = block_values.shape[2]
    slot_count = block_cols.shape[2]
    both_vals, both_cols = (
        lax.all_gather(block_values, "row", axis=1, tiled=True),
        lax.all_gather(block_cols, "row", axis=1, tiled=True),
    )
    mine_vals = block_values[:, 0]
    mine_cols = block_cols[:, 0]
    payload = (mine_vals, mine_cols)
    lower_parts = []
    lower_parts.insert(0, shift_whole(payload, 1))
    upper_parts = [shift_whole(payload, -1)]
    lower_vals = jnp.concatenate([piece[0] for piece in lower_parts], axis=0)
    lower_cols = jnp.concatenate([piece[1] for piece in lower_parts], axis=0)
    upper_vals = jnp.concatenate([piece[0] for piece in upper_parts], axis=0)
    upper_cols = jnp.concatenate([piece[1] for piece in upper_parts], axis=0)
    window_vals = jnp.concatenate([lower_vals, mine_vals, upper_vals], axis=0)
    window_cols = jnp.concatenate([lower_cols, mine_cols, upper_cols], axis=0)
    window_start = lax.axis_index("col") * band_rows - REACH
    group_size = 2

    def rows_product(local_rows):
        row_cols = jnp.take(both_cols, local_rows, axis=0)
        row_vals = jnp.take(both_vals, local_rows, axis=0)
        flat_cols = row_cols.reshape(group_size, 2 * slot_count)
        target = jnp.take(mine_cols, local_rows, axis=0)
        window_rows = jnp.where(
            flat_cols >= 0, flat_cols - window_start, REACH + local_rows[:, None]
        )
        right_vals = jnp.take(window_vals, window_rows, axis=0)
        right_cols = jnp.take(window_cols, window_rows, axis=0)
        matches = (
            (right_cols[:, :, :, None] == target[:, None, None, :])
            & (right_cols[:, :, :, None] >= 0)
            & (target[:, None, None, :] >= 0)
            & (flat_cols >= 0)[:, :, None, None]
        )
        weights = matches.astype(jnp.float32)
        left_blocks = (
            row_vals.reshape(group_size, 2, block_side, slot_count, block_side)
            .transpose(0, 1, 3, 2, 4)
            .reshape(group_size, 2 * slot_count, block_side, block_side)
        )
        partial_rows = jnp.einsum(
            "gqab,gqbe->gqae",
            left_blocks,
            right_vals,
            precision=lax.Precision.HIGHEST,
            preferred_element_type=jnp.float32,
        )
        partial_rows = partial_rows.reshape(
            group_size, 2 * slot_count, block_side, slot_count, block_side
        )
        placed = jnp.einsum(
            "gqaud,gqus->gasd",
            partial_rows,
            weights,
            precision=lax.Precision.HIGHEST,
            preferred_element_type=jnp.float32,
        )
        return placed.reshape(group_size, block_side, slot_count * block_side)

    row_groups = jnp.arange(band_rows, dtype=jnp.int32).reshape(band_rows // group_size, group_size)
    result = lax.map(rows_product, row_groups).reshape(
        band_rows, block_side, slot_count * block_side
    )
    return result[:, None]


def solution(mesh):
    in_specs = (P(("groups", "col"), "row", None, None), P(("groups", "col"), "row", None))
    out_specs = P(("groups", "col"), "row", None, None)
    return jax.shard_map(local, mesh=mesh, in_specs=in_specs, out_specs=out_specs, check_vma=False)
```

profile of v0, /device:TPU:8, one launch (start us, length us, event | category | flops | bytes accessed | tf_op | source)
XLA Modules:
  0.0 408.8 jit_solution(1503884633281895082)
XLA Ops:
  17.2 4.2 %collective-permute-start.1 = (s32[10,10]{1,0:T(8,128)S(1)}, s32[10,10]{1,0:T(8,128)S(1)}, u32[]{:S(2)}, u32[]{:S(2)}) collective-permute-start(s32[10,10]{1,0:T(8,128)S(1)} %bitcast.72), channel_id=1, source_target_pairs={{1,0},{2,1},{3,2},{4,3},{5,4},{6,5},{7,6},{9,8},{10,9},{11,10},{12... | collective-permute-start | bytes 1208 | tf_op jit(solution)/shard_map/ppermute | solution.py:12
  23.3 58.1 %collective-permute-done = s32[10,10]{1,0:T(8,128)S(1)} collective-permute-done((s32[10,10]{1,0:T(8,128)S(1)}, s32[10,10]{1,0:T(8,128)S(1)}, u32[]{:S(2)}, u32[]{:S(2)}) %collective-permute-start) | collective-permute-done | bytes 432 | tf_op jit(solution)/shard_map/ppermute | solution.py:12
  83.3 4.6 %pad_maximum_fusion = f32[30,64,640]{2,1,0:T(8,128)} fusion(f32[10,64,640]{2,1,0:T(8,128)} %collective-permute-done.3, f32[10,64,640]{2,1,0:T(8,128)} %bitcast.70, f32[10,64,640]{2,1,0:T(8,128)S(1)} %collective-permute-done.2), kind=kLoop, calls=%fused_computation.41 | loop fusion | flops 2457600 | bytes 9830400 | tf_op jit(solution)/shard_map/concatenate | solution.py:37
  87.9 314.1 %while.10 = (s32[]{:T(128)}, f32[5,2,64,640]{3,2,1,0:T(8,128)}, s32[5,2]{1,0:T(8,128)S(1)}, s32[10,2,10]{2,1,0:T(2,128)S(1)}, s32[]{:T(128)}, /*index=5*/s32[30,...) while((s32[]{:T(128)}, f32[5,2,64,640]{3,2,1,0:T(8,128)}, ...), condition=%wide.region_1.2_spmd, body=%wide.region_0.1_spmd.sunk | while | flops 1456720896 | bytes 52787484 | solution.py:84
  88.8 6.1 %gather_fusion.2 = f32[40,64,640]{2,1,0:T(8,128)} fusion(f32[30,64,640]{2,1,0:T(8,128)} %get-tuple-element.183, s32[1024]{0:T(1024)S(1)} %pad_clamp_fusion.5), kind=kCustom, calls=%fused_computation.4.clone.1 | custom fusion | bytes 13107360 | tf_op jit(solution)/shard_map/while/body/eval_jaxpr/jit(_take)/gather | solution.py:50
  98.2 24.8 %fusion.29 = f32[2,20,64,640]{2,3,1,0:T(8,128)} fusion(f32[2,20,64,64]{2,3,1,0:T(8,128)S(1)} %bitcast.65, f32[2,20,64,640]{3,2,1,0:T(8,128)} %bitcast.64, pred[2,20]{1,0:T(4,128)(4,1)S(1)} %get-tuple-element.149), kind=kOutput, calls=%fused_computation.5.clone.1 | convolution fusion | flops 1259929600 | bytes 13762600 | tf_op jit(solution)/shard_map/while/body/eval_jaxpr/gqab,gqbe->gqae/dot_general | solution.py:64
  123.0 15.4 %copy.53 = f32[2,20,64,10,64]{4,1,3,2,0:T(8,128)} copy(f32[2,20,64,10,64]{2,4,3,1,0:T(8,128)} %bitcast.63) | data formatting | bytes 13107200 | tf_op jit(solution)/shard_map/while/body/eval_jaxpr/reshape | solution.py:71
  139.8 9.6 %convolution_bitcast_fusion.2 = f32[2,64,10,64]{3,2,1,0:T(8,128)S(1)} fusion(f32[2,20,64,10,64]{4,1,3,2,0:T(8,128)} %copy.53, s32[2,10]{1,0:T(2,128)S(1)} %get-tuple-element.150, s32[2,20,10]{1,2,0:T(8,128)S(1)} %copy.55, pred[2,20]{1,0:T(4,128)(4,1)S(1)} %get-tuple-element.152, pred[2,10]{1,0:T(4,128)(4,1)S(1)} %get-tuple-element.153, ...), kind=kOutput, calls=%fused_computation.9.clone.1 | convolution fusion | flops 196624000 | bytes 6883420 | tf_op jit(solution)/shard_map/while/body/eval_jaxpr/gqaud,gqus->gasd/dot_general | solution.py:74
  151.6 6.1 %gather_fusion.2 = f32[40,64,640]{2,1,0:T(8,128)} fusion(f32[30,64,640]{2,1,0:T(8,128)} %get-tuple-element.183, s32[1024]{0:T(1024)S(1)} %pad_clamp_fusion.5), kind=kCustom, calls=%fused_computation.4.clone.1 | custom fusion | bytes 13107360 | tf_op jit(solution)/shard_map/while/body/eval_jaxpr/jit(_take)/gather | solution.py:50
  161.0 24.8 %fusion.29 = f32[2,20,64,640]{2,3,1,0:T(8,128)} fusion(f32[2,20,64,64]{2,3,1,0:T(8,128)S(1)} %bitcast.65, f32[2,20,64,640]{3,2,1,0:T(8,128)} %bitcast.64, pred[2,20]{1,0:T(4,128)(4,1)S(1)} %get-tuple-element.149), kind=kOutput, calls=%fused_computation.5.clone.1 | convolution fusion | flops 1259929600 | bytes 13762600 | tf_op jit(solution)/shard_map/while/body/eval_jaxpr/gqab,gqbe->gqae/dot_general | solution.py:64
  185.8 15.4 %copy.53 = f32[2,20,64,10,64]{4,1,3,2,0:T(8,128)} copy(f32[2,20,64,10,64]{2,4,3,1,0:T(8,128)} %bitcast.63) | data formatting | bytes 13107200 | tf_op jit(solution)/shard_map/while/body/eval_jaxpr/reshape | solution.py:71
  202.6 9.6 %convolution_bitcast_fusion.2 = f32[2,64,10,64]{3,2,1,0:T(8,128)S(1)} fusion(f32[2,20,64,10,64]{4,1,3,2,0:T(8,128)} %copy.53, s32[2,10]{1,0:T(2,128)S(1)} %get-tuple-element.150, s32[2,20,10]{1,2,0:T(8,128)S(1)} %copy.55, pred[2,20]{1,0:T(4,128)(4,1)S(1)} %get-tuple-element.152, pred[2,10]{1,0:T(4,128)(4,1)S(1)} %get-tuple-element.153, ...), kind=kOutput, calls=%fused_computation.9.clone.1 | convolution fusion | flops 196624000 | bytes 6883420 | tf_op jit(solution)/shard_map/while/body/eval_jaxpr/gqaud,gqus->gasd/dot_general | solution.py:74
  214.4 6.1 %gather_fusion.2 = f32[40,64,640]{2,1,0:T(8,128)} fusion(f32[30,64,640]{2,1,0:T(8,128)} %get-tuple-element.183, s32[1024]{0:T(1024)S(1)} %pad_clamp_fusion.5), kind=kCustom, calls=%fused_computation.4.clone.1 | custom fusion | bytes 13107360 | tf_op jit(solution)/shard_map/while/body/eval_jaxpr/jit(_take)/gather | solution.py:50
  223.8 24.8 %fusion.29 = f32[2,20,64,640]{2,3,1,0:T(8,128)} fusion(f32[2,20,64,64]{2,3,1,0:T(8,128)S(1)} %bitcast.65, f32[2,20,64,640]{3,2,1,0:T(8,128)} %bitcast.64, pred[2,20]{1,0:T(4,128)(4,1)S(1)} %get-tuple-element.149), kind=kOutput, calls=%fused_computation.5.clone.1 | convolution fusion | flops 1259929600 | bytes 13762600 | tf_op jit(solution)/shard_map/while/body/eval_jaxpr/gqab,gqbe->gqae/dot_general | solution.py:64
  248.6 15.4 %copy.53 = f32[2,20,64,10,64]{4,1,3,2,0:T(8,128)} copy(f32[2,20,64,10,64]{2,4,3,1,0:T(8,128)} %bitcast.63) | data formatting | bytes 13107200 | tf_op jit(solution)/shard_map/while/body/eval_jaxpr/reshape | solution.py:71
  265.4 9.6 %convolution_bitcast_fusion.2 = f32[2,64,10,64]{3,2,1,0:T(8,128)S(1)} fusion(f32[2,20,64,10,64]{4,1,3,2,0:T(8,128)} %copy.53, s32[2,10]{1,0:T(2,128)S(1)} %get-tuple-element.150, s32[2,20,10]{1,2,0:T(8,128)S(1)} %copy.55, pred[2,20]{1,0:T(4,128)(4,1)S(1)} %get-tuple-element.152, pred[2,10]{1,0:T(4,128)(4,1)S(1)} %get-tuple-element.153, ...), kind=kOutput, calls=%fused_computation.9.clone.1 | convolution fusion | flops 196624000 | bytes 6883420 | tf_op jit(solution)/shard_map/while/body/eval_jaxpr/gqaud,gqus->gasd/dot_general | solution.py:74
  277.2 6.1 %gather_fusion.2 = f32[40,64,640]{2,1,0:T(8,128)} fusion(f32[30,64,640]{2,1,0:T(8,128)} %get-tuple-element.183, s32[1024]{0:T(1024)S(1)} %pad_clamp_fusion.5), kind=kCustom, calls=%fused_computation.4.clone.1 | custom fusion | bytes 13107360 | tf_op jit(solution)/shard_map/while/body/eval_jaxpr/jit(_take)/gather | solution.py:50
  286.6 24.8 %fusion.29 = f32[2,20,64,640]{2,3,1,0:T(8,128)} fusion(f32[2,20,64,64]{2,3,1,0:T(8,128)S(1)} %bitcast.65, f32[2,20,64,640]{3,2,1,0:T(8,128)} %bitcast.64, pred[2,20]{1,0:T(4,128)(4,1)S(1)} %get-tuple-element.149), kind=kOutput, calls=%fused_computation.5.clone.1 | convolution fusion | flops 1259929600 | bytes 13762600 | tf_op jit(solution)/shard_map/while/body/eval_jaxpr/gqab,gqbe->gqae/dot_general | solution.py:64
  311.4 15.4 %copy.53 = f32[2,20,64,10,64]{4,1,3,2,0:T(8,128)} copy(f32[2,20,64,10,64]{2,4,3,1,0:T(8,128)} %bitcast.63) | data formatting | bytes 13107200 | tf_op jit(solution)/shard_map/while/body/eval_jaxpr/reshape | solution.py:71
  328.2 9.6 %convolution_bitcast_fusion.2 = f32[2,64,10,64]{3,2,1,0:T(8,128)S(1)} fusion(f32[2,20,64,10,64]{4,1,3,2,0:T(8,128)} %copy.53, s32[2,10]{1,0:T(2,128)S(1)} %get-tuple-element.150, s32[2,20,10]{1,2,0:T(8,128)S(1)} %copy.55, pred[2,20]{1,0:T(4,128)(4,1)S(1)} %get-tuple-element.152, pred[2,10]{1,0:T(4,128)(4,1)S(1)} %get-tuple-element.153, ...), kind=kOutput, calls=%fused_computation.9.clone.1 | convolution fusion | flops 196624000 | bytes 6883420 | tf_op jit(solution)/shard_map/while/body/eval_jaxpr/gqaud,gqus->gasd/dot_general | solution.py:74
  340.0 6.1 %gather_fusion.2 = f32[40,64,640]{2,1,0:T(8,128)} fusion(f32[30,64,640]{2,1,0:T(8,128)} %get-tuple-element.183, s32[1024]{0:T(1024)S(1)} %pad_clamp_fusion.5), kind=kCustom, calls=%fused_computation.4.clone.1 | custom fusion | bytes 13107360 | tf_op jit(solution)/shard_map/while/body/eval_jaxpr/jit(_take)/gather | solution.py:50
  349.4 24.8 %fusion.29 = f32[2,20,64,640]{2,3,1,0:T(8,128)} fusion(f32[2,20,64,64]{2,3,1,0:T(8,128)S(1)} %bitcast.65, f32[2,20,64,640]{3,2,1,0:T(8,128)} %bitcast.64, pred[2,20]{1,0:T(4,128)(4,1)S(1)} %get-tuple-element.149), kind=kOutput, calls=%fused_computation.5.clone.1 | convolution fusion | flops 1259929600 | bytes 13762600 | tf_op jit(solution)/shard_map/while/body/eval_jaxpr/gqab,gqbe->gqae/dot_general | solution.py:64
  374.2 15.4 %copy.53 = f32[2,20,64,10,64]{4,1,3,2,0:T(8,128)} copy(f32[2,20,64,10,64]{2,4,3,1,0:T(8,128)} %bitcast.63) | data formatting | bytes 13107200 | tf_op jit(solution)/shard_map/while/body/eval_jaxpr/reshape | solution.py:71
  391.0 9.6 %convolution_bitcast_fusion.2 = f32[2,64,10,64]{3,2,1,0:T(8,128)S(1)} fusion(f32[2,20,64,10,64]{4,1,3,2,0:T(8,128)} %copy.53, s32[2,10]{1,0:T(2,128)S(1)} %get-tuple-element.150, s32[2,20,10]{1,2,0:T(8,128)S(1)} %copy.55, pred[2,20]{1,0:T(4,128)(4,1)S(1)} %get-tuple-element.152, pred[2,10]{1,0:T(4,128)(4,1)S(1)} %get-tuple-element.153, ...), kind=kOutput, calls=%fused_computation.9.clone.1 | convolution fusion | flops 196624000 | bytes 6883420 | tf_op jit(solution)/shard_map/while/body/eval_jaxpr/gqaud,gqus->gasd/dot_general | solution.py:74
  (140 shorter events, 48.5 us)
Async XLA Ops:
  6.5 81.4 %all-gather.2.cloned.1.call-start = ((), (), s32[]{:S(2)}) async-start(), calls=%async_computation | async-start | bytes 4915200 | tf_op jit(solution)/shard_map/all_gather | solution.py:24
  7.3 76.0 %collective-permute-start.2 = (f32[10,64,640]{2,1,0:T(8,128)}, f32[10,64,640]{2,1,0:T(8,128)S(1)}, u32[]{:S(2)}, u32[]{:S(2)}) collective-permute-start(f32[10,64,640]{2,1,0:T(8,128)} %bitcast.68), channel_id=1, source_target_pairs={{0,1},{1,2},{2,3},{3,4},{4,5},{5,6},{6,7},{8,9},{9,10},{10,11},{11... | collective-permute-start | bytes 4915208 | tf_op jit(solution)/shard_map/ppermute | solution.py:12
  10.7 72.6 %collective-permute-start.3 = (f32[10,64,640]{2,1,0:T(8,128)}, f32[10,64,640]{2,1,0:T(8,128)}, u32[]{:S(2)}, u32[]{:S(2)}) collective-permute-start(f32[10,64,640]{2,1,0:T(8,128)} %bitcast.69), channel_id=1, source_target_pairs={{1,0},{2,1},{3,2},{4,3},{5,4},{6,5},{7,6},{9,8},{10,9},{11,10},{12... | collective-permute-start | bytes 4915208 | tf_op jit(solution)/shard_map/ppermute | solution.py:12
  14.7 66.7 %collective-permute-start = (s32[10,10]{1,0:T(8,128)S(1)}, s32[10,10]{1,0:T(8,128)S(1)}, u32[]{:S(2)}, u32[]{:S(2)}) collective-permute-start(s32[10,10]{1,0:T(8,128)S(1)} %bitcast.71), channel_id=1, source_target_pairs={{0,1},{1,2},{2,3},{3,4},{4,5},{5,6},{6,7},{8,9},{9,10},{10,11},{11... | collective-permute-start | bytes 1208 | tf_op jit(solution)/shard_map/ppermute | solution.py:12
  17.2 66.1 %collective-permute-start.1 = (s32[10,10]{1,0:T(8,128)S(1)}, s32[10,10]{1,0:T(8,128)S(1)}, u32[]{:S(2)}, u32[]{:S(2)}) collective-permute-start(s32[10,10]{1,0:T(8,128)S(1)} %bitcast.72), channel_id=1, source_target_pairs={{1,0},{2,1},{3,2},{4,3},{5,4},{6,5},{7,6},{9,8},{10,9},{11,10},{12... | collective-permute-start | bytes 1208 | tf_op jit(solution)/shard_map/ppermute | solution.py:12
Sparse Core Ops, SparseCore 0:
  8.9 13.7 all-gather.1
where the time goes:
time: 411 us; the launch traced here: 409 us
  matrix products  172 us (42%)
  local copies, waits for them, and re-layouts  140 us (34%)
  waiting for transfers between devices  60.7 us (15%)
  starting transfers between devices  13.5 us (3%)
  between operations  13.5 us (3%)
  other arithmetic  7.14 us (2%)
    dot_general x5, matrix products, rows_product(): jnp.einsum('gqab,gqbe->gqae', left_blocks, right_vals, precision=lax.Prec...  124 us
    reshape x5, local copies, waits for them, and re-layouts, rows_product(): partial_rows.reshape(group_size, 2 * slot_count, block_side, slot_count,...  77 us
    ppermute x4, waiting for transfers between devices, shifted(): return lax.ppermute(shard, axis, pairs)  60 us
    dot_general x5, matrix products, rows_product(): jnp.einsum('gqaud,gqus->gasd', partial_rows, weights, precision=lax.Preci...  48.2 us
    gather x5, local copies, waits for them, and re-layouts, rows_product(): right_vals = jnp.take(window_vals, window_rows, axis=0)  30.5 us
    gather x10, local copies, waits for them, and re-layouts, rows_product(): row_vals = jnp.take(both_vals, local_rows, axis=0)  14.6 us
    ppermute x4, starting transfers between devices, shifted(): return lax.ppermute(shard, axis, pairs)  13.5 us
  transfers between devices with their start and end apart: 5, of which 2 were waited for; matrix products, arithmetic and copies ran while one was open for 1% of the time, Pallas kernels for 0%

commit v1 on v0

v1 whole, which is shorter than its diff:
```python
import functools

import jax
import jax.numpy as jnp
from jax import lax
from jax.experimental import pallas as pl
from jax.experimental.pallas import tpu as pltpu
from jax.sharding import PartitionSpec as P

REACH = 10
CHUNK = 2
OWN_AT, X_AT, F_AT, OUT_AT = 0, 32, 64, 96
MESH = pl.DeviceIdType.MESH


def picked(codes, tiles):
    high = (lax.broadcasted_iota(jnp.int32, (8, 128), 1) >= 64).astype(jnp.int32)
    kept, turned = codes - high, codes + high
    x = jnp.zeros((8, 8, 128), jnp.float32)
    for u, (plain, rolled) in enumerate(tiles):
        x = jnp.where((kept == 2 * u)[None], plain, x)
        x = jnp.where((turned == 2 * u + 1)[None], rolled, x)
    return x


def rolled(x):
    return pltpu.roll(x.reshape(64, 128), 64, 1).reshape(8, 8, 128)


def low_half(shape):
    return lax.broadcasted_iota(jnp.int32, shape, len(shape) - 1) < 64


def pair(low, low_at, high, high_at):
    first = jnp.broadcast_to(low[:, low_at:low_at + 1], (8, 128))
    second = jnp.broadcast_to(high[:, high_at:high_at + 1], (8, 128))
    return jnp.where(low_half((8, 128)), first, second)


def split(x):
    x = x.reshape(64, 128)
    hi = x.astype(jnp.bfloat16)
    return hi, (x - hi.astype(jnp.float32)).astype(jnp.bfloat16)


def kernel(
    n_col, band, slots, vals, inv, out,
    both, x_buf, f_buf, stage, b_hi, b_lo, a_hi, a_lo, acc, inv_o, inv_x, inv_f,
    x_send, x_recv, f_send, f_recv, c_sem, t_send, t_recv, l_sem,
):
    g, p, c = lax.axis_index("groups"), lax.axis_index("row"), lax.axis_index("col")
    chunks = band // CHUNK
    tiles = acc.shape[0]
    k_tiles = a_hi.shape[0]
    odd = lax.rem(c, 2)
    x_peer = c + 1 - 2 * odd
    f_to, f_from = c + 2 - 4 * odd, c - 2 + 4 * odd
    has_to = (f_to >= 0) & (f_to < n_col)
    has_from = (f_from >= 0) & (f_from < n_col)
    core_id, x_id = (g, 1 - p, c), (g, p, x_peer)
    to_id = (g, p, jnp.clip(f_to, 0, n_col - 1))
    from_id = (g, p, jnp.clip(f_from, 0, n_col - 1))

    barrier = pltpu.get_barrier_semaphore()
    for peer in (core_id, x_id):
        pl.semaphore_signal(barrier, inc=1, device_id=peer, device_id_type=MESH)

    @pl.when(has_to)
    def _():
        pl.semaphore_signal(barrier, inc=1, device_id=to_id, device_id_type=MESH)

    @pl.when(has_from)
    def _():
        pl.semaphore_signal(barrier, inc=1, device_id=from_id, device_id_type=MESH)

    pl.semaphore_wait(barrier, 2 + has_to.astype(jnp.int32) + has_from.astype(jnp.int32))

    def remote(src, dst, send, recv, device):
        return pltpu.make_async_remote_copy(
            src_ref=src, dst_ref=dst, send_sem=send, recv_sem=recv,
            device_id=device, device_id_type=MESH,
        )

    def rows(ch):
        return pl.ds(ch * CHUNK, CHUNK)

    def x_copy(ch):
        return remote(vals.at[rows(ch), 0], x_buf.at[rows(ch)], x_send.at[ch], x_recv.at[ch], x_id)

    def f_copy(ch):
        return remote(x_buf.at[rows(ch)], f_buf.at[rows(ch)], f_send.at[ch], f_recv.at[ch], to_id)

    tab_c = remote(inv, inv_o, t_send.at[0], t_recv.at[0], core_id)
    tab_x = remote(inv, inv_x, t_send.at[1], t_recv.at[1], x_id)
    tab_f = remote(inv_x, inv_f, t_send.at[2], t_recv.at[2], to_id)
    core = remote(vals.at[:, 0], both.at[p], c_sem.at[0], c_sem.at[1], core_id)
    own = pltpu.make_async_copy(vals.at[:, 0], both.at[p], l_sem)
    tab_x.start()
    tab_c.start()
    x_copy(0).start()
    core.start()
    own.start()
    for ch in range(1, chunks):
        x_copy(ch).start()

    acc[...] = jnp.zeros_like(acc)
    own.wait()
    core.wait()
    tab_c.wait()
    tab_x.wait()

    @pl.when(has_to)
    def _():
        tab_f.start()

    def a_row(i, carry):
        at = pl.ds(pl.multiple_of(i * 64, 64), 64)
        low = low_half((8, 8, 128))
        held = []
        for u in range(slots // 2):
            even = both[0, i, :, u * 128:(u + 1) * 128].reshape(8, 8, 128)
            odd = both[1, i, :, u * 128:(u + 1) * 128].reshape(8, 8, 128)
            held.append((jnp.where(low, even, odd), rolled(jnp.where(low, odd, even))))
        mine, other = inv[pl.ds(i, 1), :], inv_o[pl.ds(i, 1), :]
        first = jnp.where(p == 0, mine, other)
        second = jnp.where(p == 0, other, mine)
        for t in range(k_tiles):
            hi, lo = split(picked(pair(first, OWN_AT + t, second, OWN_AT + t), held))
            a_hi[t, at, :] = hi
            a_lo[t, at, :] = lo
        return carry

    lax.fori_loop(0, band, a_row, 0)

    def multiply(ch, table, first, k_tile):
        for r in range(CHUNK):
            codes = table[pl.ds(ch * CHUNK + r, 1), :]
            held = []
            for u in range(slots // 2):
                tile = stage[r, :, u * 128:(u + 1) * 128].reshape(8, 8, 128)
                held.append((tile, rolled(tile)))
            for t in range(tiles):
                at = first + 2 * t
                hi, lo = split(picked(pair(codes, at, codes, at + 1), held))
                b_hi[r * 64:(r + 1) * 64, t * 128:(t + 1) * 128] = hi
                b_lo[r * 64:(r + 1) * 64, t * 128:(t + 1) * 128] = lo
        left_hi = a_hi[k_tile]
        left = jnp.concatenate([left_hi, left_hi, a_lo[k_tile]], axis=1)
        for t in range(0, tiles, 2):
            at = slice(t * 128, (t + 2) * 128)
            right_hi = b_hi[:, at]
            right = jnp.concatenate([right_hi, b_lo[:, at], right_hi], axis=0)
            part = jnp.dot(left, right, preferred_element_type=jnp.float32)
            acc[t] += part[:, :128]
            acc[t + 1] += part[:, 128:]

    half = band // 2
    x_shift = half * (1 - 2 * odd)
    own_tile = REACH // 2
    x_tile = own_tile + x_shift
    f_tile = own_tile - x_shift

    def x_wait(ch):
        x_copy(ch).wait_recv()

        @pl.when(has_to)
        def _():
            f_copy(ch).start()

    def own_step(ch, carry):
        x_wait(ch)
        stage[...] = both[p, rows(ch)]
        multiply(ch, inv, OWN_AT, own_tile + ch)
        return carry

    lax.fori_loop(0, chunks, own_step, 0)

    def x_step(ch, carry):
        stage[...] = x_buf[rows(ch)]
        multiply(ch, inv_x, X_AT, x_tile + ch)
        return carry

    lax.fori_loop(0, chunks, x_step, 0)

    @pl.when(has_from)
    def _():
        tab_f.wait_recv()

        def f_step(ch, carry):
            f_copy(ch).wait_recv()
            stage[...] = f_buf[rows(ch)]
            multiply(ch, inv_f, F_AT, f_tile + ch)
            return carry

        lax.fori_loop(0, chunks, f_step, 0)

    def out_row(i, carry):
        at = pl.ds(pl.multiple_of(i * 64, 64), 64)
        held = []
        for u in range(tiles):
            tile = acc[u, at, :].reshape(8, 8, 128)
            held.append((tile, rolled(tile)))
        codes = inv[pl.ds(i, 1), :]
        for t in range(slots // 2):
            put = OUT_AT + 2 * t
            x = picked(pair(codes, put, codes, put + 1), held)
            out[i, 0, :, t * 128:(t + 1) * 128] = x.reshape(64, 128)
        return carry

    lax.fori_loop(0, band, out_row, 0)

    for ch in range(chunks):
        x_copy(ch).wait_send()

    @pl.when(has_to)
    def _():
        tab_f.wait_send()
        for ch in range(chunks):
            f_copy(ch).wait_send()


def local(n_col, block_values, block_cols):
    band, _, side, _ = block_values.shape
    cols = block_cols[:, 0]
    slots = cols.shape[1]
    col = lax.axis_index("col")
    base = col * band - REACH + lax.axis_index("row")
    shift = (band // 2) * (1 - 2 * lax.rem(col, 2))
    places = jnp.arange(32, dtype=jnp.int32)
    views = base + 2 * jnp.concatenate([places, places + shift, places - shift])
    found = (cols[:, :, None] == views[None, None, :]) & (cols >= 0)[:, :, None]
    inv = jnp.max(
        jnp.where(found, jnp.arange(slots, dtype=jnp.int32)[None, :, None], -1), axis=1
    )
    where_to = jnp.where(cols >= 0, (cols - base) >> 1, -1)
    rows = -(-band // 8) * 8
    inv = jnp.concatenate([inv, where_to], axis=1)
    inv = jnp.pad(inv, ((0, rows - band), (0, 128 - inv.shape[1])))
    k_tiles = (2 * REACH + band) // 2
    tiles = (k_tiles + 1) // 2
    chunks = band // CHUNK
    dma = pltpu.SemaphoreType.DMA
    return pl.pallas_call(
        functools.partial(kernel, n_col, band, slots),
        out_shape=jax.ShapeDtypeStruct(block_values.shape, jnp.float32),
        in_specs=[
            pl.BlockSpec(memory_space=pl.ANY),
            pl.BlockSpec(memory_space=pltpu.VMEM),
        ],
        out_specs=pl.BlockSpec(memory_space=pltpu.VMEM),
        scratch_shapes=[
            pltpu.VMEM((2, band, side, slots * side), jnp.float32),
            pltpu.VMEM((band, side, slots * side), jnp.float32),
            pltpu.VMEM((band, side, slots * side), jnp.float32),
            pltpu.VMEM((CHUNK, side, slots * side), jnp.float32),
            pltpu.VMEM((CHUNK * side, tiles * 128), jnp.bfloat16),
            pltpu.VMEM((CHUNK * side, tiles * 128), jnp.bfloat16),
            pltpu.VMEM((k_tiles, band * side, 128), jnp.bfloat16),
            pltpu.VMEM((k_tiles, band * side, 128), jnp.bfloat16),
            pltpu.VMEM((tiles, band * side, 128), jnp.float32),
            pltpu.VMEM((rows, 128), jnp.int32),
            pltpu.VMEM((rows, 128), jnp.int32),
            pltpu.VMEM((rows, 128), jnp.int32),
            dma((chunks,)), dma((chunks,)), dma((chunks,)), dma((chunks,)),
            dma((2,)), dma((3,)), dma((3,)), dma,
        ],
        compiler_params=pltpu.CompilerParams(
            collective_id=0, has_side_effects=True, vmem_limit_bytes=48 * 1024 * 1024
        ),
    )(block_values, inv)


def solution(mesh):
    in_specs = (P(("groups", "col"), "row", None, None), P(("groups", "col"), "row", None))
    out_specs = P(("groups", "col"), "row", None, None)
    return jax.shard_map(
        functools.partial(local, mesh.shape["col"]),
        mesh=mesh, in_specs=in_specs, out_specs=out_specs, check_vma=False,
    )
```

time: 411 us -> 60.5 us (0.15)
  matrix products: 172 us -> 0 us
  local copies, waits for them, and re-layouts: 140 us -> 3.3 us
  waiting for transfers between devices: 60.7 us -> 0 us
  Pallas kernels: 0 us -> 55.2 us
  starting transfers between devices: 13.5 us -> 0 us
  between operations: 13.5 us -> 0.02 us
  other arithmetic: 7.14 us -> 1.67 us
    dot_general x10 -> x0, matrix products: 172 us -> none  [the longest x5 124 us: rows_product(): jnp.einsum('gqab,gqbe->gqae', left_blocks, right_vals, precision=lax.Prec...]
    reshape x5 -> x0, local copies, waits for them, and re-layouts: 77 us -> none  [rows_product(): partial_rows.reshape(group_size, 2 * slot_count, block_side, slot_count,...]
    ppermute x4 -> x0, waiting for transfers between devices: 60 us -> none  [shifted(): return lax.ppermute(shard, axis, pairs)]
    pallas_call x0 -> x1, Pallas kernels: none -> 55.2 us  [local(): pl.pallas_call(functools.partial(kernel, n_col, band, slots), out_shape=j...]
    gather x50 -> x0, local copies, waits for them, and re-layouts: 55.2 us -> none  [the longest x5 30.5 us: rows_product(): right_vals = jnp.take(window_vals, window_rows, axis=0)]
    ppermute x4 -> x0, starting transfers between devices: 13.5 us -> none  [shifted(): return lax.ppermute(shard, axis, pairs)]
    dynamic_update_slice x10 -> x0, local copies, waits for them, and re-layouts: 4.82 us -> none  [local(): lax.map(rows_product, row_groups)]
    concatenate x2 -> x1, other arithmetic: 4.6 us -> 0.08 us  [local(): inv = jnp.concatenate([inv, where_to], axis=1)]
  transfers between devices with their start and end apart: 5 -> 0, of which waited for: 2 -> 0; matrix products, arithmetic and copies ran while one was open for 1% -> 0% of each run, Pallas kernels for 0% -> 0%
where the time goes in v1:
time: 60.5 us; the launch traced here: 60.2 us
  Pallas kernels  55.2 us (91%)
  local copies, waits for them, and re-layouts  3.3 us (5%)
  other arithmetic  1.67 us (3%)
    pallas_call x1, Pallas kernels, local(): pl.pallas_call(functools.partial(kernel, n_col, band, slots), out_shape=j...  55.2 us
    unnamed x4, local copies, waits for them, and re-layouts  3.29 us

profile of v1, /device:TPU:8, one launch (start us, length us, event | category | flops | bytes accessed | tf_op | source)
XLA Modules:
  0.0 60.2 jit_solution(12540753491601333896)
XLA Ops:
  0.0 0.1 fusion
  0.1 0.7 %broadcast_compare_fusion = pred[10,10]{1,0:T(8,128)(4,1)S(1)} fusion(s32[10,1,10]{2,1,0:T(1,128)} %param.3), kind=kLoop, calls=%fused_computation.4 | loop fusion | flops 100 | bytes 500 | tf_op jit(solution)/shard_map/ge | solution.py:231
  0.8 0.7 %shift-right-arithmetic_select_fusion = s32[10,10]{1,0:T(8,128)S(1)} fusion(s32[]{:T(128)S(6)} %add.24, s32[10,1,10]{2,1,0:T(1,128)} %param.3), kind=kLoop, calls=%fused_computation.3 | loop fusion | flops 400 | bytes 804 | tf_op jit(solution)/shard_map/jit(_where)/select_n | solution.py:235
  1.5 0.7 %copy.9 = s32[10,1,10]{2,0,1:T(8,128)S(1)} copy(s32[10,1,10]{2,1,0:T(1,128)} %param.3) | data formatting | bytes 800
  2.2 0.1 select_reduce_fusion
  2.3 0.1 pad_add_fusion
  2.4 0.0 copy-start
  2.4 1.4 %copy-done = f32[10,1,64,640]{3,2,1,0:T(8,128)S(1)} copy-done((f32[10,1,64,640]{3,2,1,0:T(8,128)S(1)}, f32[10,1,64,640]{3,2,1,0:T(8,128)}, u32[]{:S(2)}) %copy-start) | copy-done | bytes 1638424
  3.8 55.2 %shard_map.28 = f32[10,1,64,640]{3,2,1,0:T(8,128)S(1)} custom-call(f32[10,1,64,640]{3,2,1,0:T(8,128)S(1)} %copy-done, s32[16,128]{1,0:T(8,128)S(1)} %pad.4.inv), custom_call_target="tpu_custom_call" | custom-call | tf_op jit(solution)/shard_map/pallas_call | solution.py:243
  59.1 1.2 %copy.11 = f32[10,1,64,640]{3,2,1,0:T(8,128)} copy(f32[10,1,64,640]{3,2,1,0:T(8,128)S(1)} %shard_map.28) | data formatting | bytes 3276800
  (3 shorter events, 0.0 us)
Async XLA Ops:
  2.4 1.4 %copy-start = (f32[10,1,64,640]{3,2,1,0:T(8,128)S(1)}, f32[10,1,64,640]{3,2,1,0:T(8,128)}, u32[]{:S(2)}) copy-start(f32[10,1,64,640]{3,2,1,0:T(8,128)} %vals.1) | copy-start | bytes 4915204

commit v2 on v1

v2 whole, which is shorter than its diff:
```python
import functools

import jax
import jax.numpy as jnp
from jax import lax
from jax.experimental import pallas as pl
from jax.experimental.pallas import tpu as pltpu
from jax.sharding import PartitionSpec as P

REACH = 10
CHUNK = 2
OWN_AT, X_AT, F_AT = 0, 32, 64
MESH = pl.DeviceIdType.MESH


def picked(codes, tiles):
    high = (lax.broadcasted_iota(jnp.int32, (8, 128), 1) >= 64).astype(jnp.int32)
    kept, turned = codes - high, codes + high
    x = jnp.zeros((8, 8, 128), jnp.float32)
    for u, (plain, rolled) in enumerate(tiles):
        x = jnp.where((kept == 2 * u)[None], plain, x)
        x = jnp.where((turned == 2 * u + 1)[None], rolled, x)
    return x


def rolled(x):
    return pltpu.roll(x.reshape(64, 128), 64, 1).reshape(8, 8, 128)


def low_half(shape):
    return lax.broadcasted_iota(jnp.int32, shape, len(shape) - 1) < 64


def pair(low, low_at, high, high_at):
    first = jnp.broadcast_to(low[:, low_at:low_at + 1], (8, 128))
    second = jnp.broadcast_to(high[:, high_at:high_at + 1], (8, 128))
    return jnp.where(low_half((8, 128)), first, second)


def split(x):
    x = x.reshape(64, 128)
    hi = x.astype(jnp.bfloat16)
    return hi, (x - hi.astype(jnp.float32)).astype(jnp.bfloat16)


def kernel(
    n_col, band, slots, vals, cols, out,
    both, x_buf, f_buf, stage, b_hi, b_lo, a_hi, a_lo, acc, cols_v, put_v, inv, inv_o, inv_x, inv_f,
    x_send, x_recv, f_send, f_recv, c_sem, t_send, t_recv, l_sem,
):
    g, p, c = lax.axis_index("groups"), lax.axis_index("row"), lax.axis_index("col")
    chunks = band // CHUNK
    tiles = acc.shape[0]
    k_tiles = a_hi.shape[0]
    half = band // 2
    odd = lax.rem(c, 2)
    x_peer = c + 1 - 2 * odd
    x_shift = half * (1 - 2 * odd)
    f_to, f_from = c + 2 - 4 * odd, c - 2 + 4 * odd
    has_to = (f_to >= 0) & (f_to < n_col)
    has_from = (f_from >= 0) & (f_from < n_col)
    core_id, x_id = (g, 1 - p, c), (g, p, x_peer)
    to_id = (g, p, jnp.clip(f_to, 0, n_col - 1))
    from_id = (g, p, jnp.clip(f_from, 0, n_col - 1))

    own = pltpu.make_async_copy(vals.at[:, 0], both.at[p], l_sem.at[0])
    lists = pltpu.make_async_copy(cols, cols_v, l_sem.at[1])
    lists.start()
    own.start()

    barrier = pltpu.get_barrier_semaphore()
    for peer in (core_id, x_id):
        pl.semaphore_signal(barrier, inc=1, device_id=peer, device_id_type=MESH)

    @pl.when(has_to)
    def _():
        pl.semaphore_signal(barrier, inc=1, device_id=to_id, device_id_type=MESH)

    @pl.when(has_from)
    def _():
        pl.semaphore_signal(barrier, inc=1, device_id=from_id, device_id_type=MESH)

    lists.wait()
    column = cols_v[:, 0, :]
    base = c * band - REACH + p
    lane = lax.broadcasted_iota(jnp.int32, (band, 128), 1)
    view = lane >> 5
    moved = jnp.where(view == 1, x_shift, jnp.where(view == 2, -x_shift, 0))
    wanted = base + 2 * ((lane & 31) + moved)
    codes = jnp.full((band, 128), -1, jnp.int32)
    for slot in range(slots):
        held = jnp.broadcast_to(column[:, slot:slot + 1], (band, 128))
        codes = jnp.where((held == wanted) & (held >= 0), slot, codes)
    inv[...] = jnp.full(inv.shape, -1, jnp.int32)
    inv[:band, :] = codes
    put_v[...] = jnp.where(column >= 0, (column - base) >> 1, -1)
    pl.semaphore_wait(barrier, 2 + has_to.astype(jnp.int32) + has_from.astype(jnp.int32))

    def remote(src, dst, send, recv, device):
        return pltpu.make_async_remote_copy(
            src_ref=src, dst_ref=dst, send_sem=send, recv_sem=recv,
            device_id=device, device_id_type=MESH,
        )

    def x_copy(row):
        return remote(vals.at[row, 0], x_buf.at[row], x_send.at[row], x_recv.at[row], x_id)

    def f_copy(row):
        return remote(x_buf.at[row], f_buf.at[row], f_send.at[row], f_recv.at[row], to_id)

    def sent_row(h):
        return jnp.where(odd == 1, band - 1 - h, h)

    def got_row(h):
        return jnp.where(odd == 1, h, band - 1 - h)

    def got_chunk(m):
        return jnp.where(odd == 1, m, chunks - 1 - m)

    tab_c = remote(inv, inv_o, t_send.at[0], t_recv.at[0], core_id)
    tab_x = remote(inv, inv_x, t_send.at[1], t_recv.at[1], x_id)
    tab_f = remote(inv_x, inv_f, t_send.at[2], t_recv.at[2], to_id)
    core = remote(vals.at[:, 0], both.at[p], c_sem.at[0], c_sem.at[1], core_id)
    tab_x.start()
    tab_c.start()
    x_copy(sent_row(0)).start()
    core.start()
    for h in range(1, band):
        x_copy(sent_row(h)).start()

    acc[...] = jnp.zeros_like(acc)
    own.wait()
    tab_x.wait()

    @pl.when(has_to)
    def _():
        tab_f.start()

    core.wait()
    tab_c.wait()

    def a_row(i, carry):
        at = pl.ds(pl.multiple_of(i * 64, 64), 64)
        low = low_half((8, 8, 128))
        held = []
        for u in range(slots // 2):
            even = both[0, i, :, u * 128:(u + 1) * 128].reshape(8, 8, 128)
            odd = both[1, i, :, u * 128:(u + 1) * 128].reshape(8, 8, 128)
            held.append((jnp.where(low, even, odd), rolled(jnp.where(low, odd, even))))
        mine, other = inv[pl.ds(i, 1), :], inv_o[pl.ds(i, 1), :]
        first = jnp.where(p == 0, mine, other)
        second = jnp.where(p == 0, other, mine)
        for t in range(k_tiles):
            hi, lo = split(picked(pair(first, OWN_AT + t, second, OWN_AT + t), held))
            a_hi[t, at, :] = hi
            a_lo[t, at, :] = lo
        return carry

    lax.fori_loop(0, band, a_row, 0)

    def spread(chunk, table, first, load):
        for r in range(CHUNK):
            stage[r] = load(chunk * CHUNK + r)
            codes = table[pl.ds(chunk * CHUNK + r, 1), :]
            held = []
            for u in range(slots // 2):
                tile = stage[r, :, u * 128:(u + 1) * 128].reshape(8, 8, 128)
                held.append((tile, rolled(tile)))
            for t in range(tiles):
                at = first + 2 * t
                hi, lo = split(picked(pair(codes, at, codes, at + 1), held))
                b_hi[r * 64:(r + 1) * 64, t * 128:(t + 1) * 128] = hi
                b_lo[r * 64:(r + 1) * 64, t * 128:(t + 1) * 128] = lo

    def multiply(k_tile, at):
        left_hi = a_hi[k_tile, at, :]
        left = jnp.concatenate([left_hi, left_hi, a_lo[k_tile, at, :]], axis=1)
        for t in range(0, tiles, 2):
            wide = slice(t * 128, (t + 2) * 128)
            right_hi = b_hi[:, wide]
            right = jnp.concatenate([right_hi, b_lo[:, wide], right_hi], axis=0)
            part = jnp.dot(left, right, preferred_element_type=jnp.float32)
            acc[t, at, :] += part[:, :128]
            acc[t + 1, at, :] += part[:, 128:]

    own_tile = REACH // 2
    everything = pl.ds(0, band * 64)

    def forward(h):
        row = got_row(h)
        x_copy(row).wait_recv()

        @pl.when(has_to)
        def _():
            f_copy(row).start()

    def from_relay(row):
        f_copy(row).wait_recv()
        return f_buf[row]

    def relay_chunk(m):
        spread(got_chunk(m), inv_f, F_AT, from_relay)
        return own_tile - x_shift + got_chunk(m)

    def step(m, carry):
        forward(CHUNK * m)
        spread(m, inv, OWN_AT, lambda row: both[p, row])
        multiply(own_tile + m, everything)
        for r in range(1, CHUNK):
            forward(CHUNK * m + r)
        spread(got_chunk(m), inv_x, X_AT, lambda row: x_buf[row])
        multiply(own_tile + x_shift + got_chunk(m), everything)

        @pl.when(has_from & (m >= 1))
        def _():
            @pl.when(m == 1)
            def _():
                tab_f.wait_recv()

            multiply(relay_chunk(m - 1), everything)

        return carry

    lax.fori_loop(0, chunks, step, 0)

    def out_row(i, carry):
        at = pl.ds(pl.multiple_of(i * 64, 64), 64)
        held = []
        for u in range(tiles):
            tile = acc[u, at, :].reshape(8, 8, 128)
            held.append((tile, rolled(tile)))
        codes = put_v[pl.ds(i, 1), :]
        for t in range(slots // 2):
            put = 2 * t
            x = picked(pair(codes, put, codes, put + 1), held)
            out[i, 0, :, t * 128:(t + 1) * 128] = x.reshape(64, 128)
        return carry

    last = got_chunk(chunks - 1) * CHUNK
    start = jnp.where(odd == 1, 0, CHUNK)
    lax.fori_loop(start, start + band - CHUNK, out_row, 0)

    @pl.when(has_from)
    def _():
        k_tile = relay_chunk(chunks - 1)
        multiply(k_tile, pl.ds(pl.multiple_of(last * 64, 128), CHUNK * 64))

    lax.fori_loop(last, last + CHUNK, out_row, 0)

    for row in range(band):
        x_copy(row).wait_send()

    @pl.when(has_to)
    def _():
        tab_f.wait_send()
        for row in range(band):
            f_copy(row).wait_send()


def local(n_col, block_values, block_cols):
    band, _, side, _ = block_values.shape
    slots = block_cols.shape[2]
    rows = -(-band // 8) * 8
    k_tiles = (2 * REACH + band) // 2
    tiles = (k_tiles + 1) // 2
    dma = pltpu.SemaphoreType.DMA
    return pl.pallas_call(
        functools.partial(kernel, n_col, band, slots),
        out_shape=jax.ShapeDtypeStruct(block_values.shape, jnp.float32),
        in_specs=[
            pl.BlockSpec(memory_space=pltpu.HBM),
            pl.BlockSpec(memory_space=pltpu.HBM),
        ],
        out_specs=pl.BlockSpec(memory_space=pltpu.VMEM),
        scratch_shapes=[
            pltpu.VMEM((2, band, side, slots * side), jnp.float32),
            pltpu.VMEM((band, side, slots * side), jnp.float32),
            pltpu.VMEM((band, side, slots * side), jnp.float32),
            pltpu.VMEM((CHUNK, side, slots * side), jnp.float32),
            pltpu.VMEM((CHUNK * side, tiles * 128), jnp.bfloat16),
            pltpu.VMEM((CHUNK * side, tiles * 128), jnp.bfloat16),
            pltpu.VMEM((k_tiles, band * side, 128), jnp.bfloat16),
            pltpu.VMEM((k_tiles, band * side, 128), jnp.bfloat16),
            pltpu.VMEM((tiles, band * side, 128), jnp.float32),
            pltpu.VMEM(block_cols.shape, jnp.int32),
            pltpu.VMEM((band, slots), jnp.int32),
            pltpu.VMEM((rows, 128), jnp.int32),
            pltpu.VMEM((rows, 128), jnp.int32),
            pltpu.VMEM((rows, 128), jnp.int32),
            pltpu.VMEM((rows, 128), jnp.int32),
            dma((band,)), dma((band,)), dma((band,)), dma((band,)),
            dma((2,)), dma((3,)), dma((3,)), dma((2,)),
        ],
        compiler_params=pltpu.CompilerParams(
            collective_id=0, has_side_effects=True, vmem_limit_bytes=48 * 1024 * 1024
        ),
    )(block_values, block_cols)


def solution(mesh):
    in_specs = (P(("groups", "col"), "row", None, None), P(("groups", "col"), "row", None))
    out_specs = P(("groups", "col"), "row", None, None)
    return jax.shard_map(
        functools.partial(local, mesh.shape["col"]),
        mesh=mesh, in_specs=in_specs, out_specs=out_specs, check_vma=False,
    )
```

time: 60.5 us -> 52.1 us (0.86); the launches traced: 60.2 us -> 51.1 us
  Pallas kernels: 55.2 us -> 47.8 us
  other arithmetic: 1.67 us -> 0 us
    pallas_call x1, Pallas kernels: 55.2 us -> 47.8 us  [local(): pl.pallas_call(functools.partial(kernel, n_col, band, slots), out_shape=j...]
    ge x1 -> x0, other arithmetic: 0.69 us -> none  [local(): found = (cols[:, :, None] == views[None, None, :]) & (cols >= 0)[:, :, None]]
    select_n x1 -> x0, other arithmetic: 0.69 us -> none  [local(): where_to = jnp.where(cols >= 0, cols - base >> 1, -1)]
    unnamed x4 -> x5, local copies, waits for them, and re-layouts: 3.29 us -> 3.29 us
where the time goes in v2:
time: 52.1 us; the launch traced here: 51.1 us
  Pallas kernels  47.8 us (92%)
  local copies, waits for them, and re-layouts  3.29 us (6%)
    pallas_call x1, Pallas kernels, local(): pl.pallas_call(functools.partial(kernel, n_col, band, slots), out_shape=j...  47.8 us
    unnamed x5, local copies, waits for them, and re-layouts  3.29 us

profile of v2, /device:TPU:8, one launch (start us, length us, event | category | flops | bytes accessed | tf_op | source)
XLA Modules:
  0.0 51.1 jit_solution(2895520253224520452)
XLA Ops:
  0.0 0.0 copy-start
  0.0 1.4 %copy-done = f32[10,1,64,640]{3,2,1,0:T(8,128)S(1)} copy-done((f32[10,1,64,640]{3,2,1,0:T(8,128)S(1)}, f32[10,1,64,640]{3,2,1,0:T(8,128)}, u32[]{:S(2)}) %copy-start) | copy-done | bytes 1638424
  1.4 0.0 copy-start.1
  1.4 0.7 %copy-done.1 = s32[10,1,10]{2,1,0:T(1,128)S(1)} copy-done((s32[10,1,10]{2,1,0:T(1,128)S(1)}, s32[10,1,10]{2,1,0:T(1,128)}, u32[]{:S(2)}) %copy-start.1) | copy-done | bytes 424
  2.1 47.8 %shard_map.28 = f32[10,1,64,640]{3,2,1,0:T(8,128)S(1)} custom-call(f32[10,1,64,640]{3,2,1,0:T(8,128)S(1)} %copy-done, s32[10,1,10]{2,1,0:T(1,128)S(1)} %copy-done.1), custom_call_target="tpu_custom_call" | custom-call | tf_op jit(solution)/shard_map/pallas_call | solution.py:267
  50.0 1.2 %copy.4 = f32[10,1,64,640]{3,2,1,0:T(8,128)} copy(f32[10,1,64,640]{3,2,1,0:T(8,128)S(1)} %shard_map.28) | data formatting | bytes 3276800
Async XLA Ops:
  0.0 1.4 %copy-start = (f32[10,1,64,640]{3,2,1,0:T(8,128)S(1)}, f32[10,1,64,640]{3,2,1,0:T(8,128)}, u32[]{:S(2)}) copy-start(f32[10,1,64,640]{3,2,1,0:T(8,128)} %vals.1) | copy-start | bytes 4915204
  1.4 0.7 %copy-start.1 = (s32[10,1,10]{2,1,0:T(1,128)S(1)}, s32[10,1,10]{2,1,0:T(1,128)}, u32[]{:S(2)}) copy-start(s32[10,1,10]{2,1,0:T(1,128)} %cols.1) | copy-start | bytes 1204

commit v3 on v2

--- a/solution.py
+++ b/solution.py
@@ -9,6 +9,8 @@
 
 REACH = 10
 CHUNK = 2
+PIECE = 32
+PARTS = 2
 OWN_AT, X_AT, F_AT = 0, 32, 64
 MESH = pl.DeviceIdType.MESH
 
@@ -45,7 +47,7 @@
 
 def kernel(
     n_col, band, slots, vals, cols, out,
-    both, x_buf, f_buf, stage, b_hi, b_lo, a_hi, a_lo, acc, cols_v, put_v, inv, inv_o, inv_x, inv_f,
+    both, x_buf, f_buf, out_v, stage, b_hi, b_lo, a_hi, a_lo, acc, cols_v, put_v, inv, inv_o, inv_x, inv_f,
     x_send, x_recv, f_send, f_recv, c_sem, t_send, t_recv, l_sem,
 ):
     g, p, c = lax.axis_index("groups"), lax.axis_index("row"), lax.axis_index("col")
@@ -102,11 +104,17 @@
             device_id=device, device_id_type=MESH,
         )
 
-    def x_copy(row):
-        return remote(vals.at[row, 0], x_buf.at[row], x_send.at[row], x_recv.at[row], x_id)
-
-    def f_copy(row):
-        return remote(x_buf.at[row], f_buf.at[row], f_send.at[row], f_recv.at[row], to_id)
+    def x_copy(row, part):
+        at, sem = pl.ds(part * PIECE, PIECE), row * PARTS + part
+        return remote(
+            vals.at[row, 0, at], x_buf.at[row, at], x_send.at[sem], x_recv.at[sem], x_id
+        )
+
+    def f_copy(row, part):
+        at, sem = pl.ds(part * PIECE, PIECE), row * PARTS + part
+        return remote(
+            x_buf.at[row, at], f_buf.at[row, at], f_send.at[sem], f_recv.at[sem], to_id
+        )
 
     def sent_row(h):
         return jnp.where(odd == 1, band - 1 - h, h)
@@ -123,10 +131,10 @@
     core = remote(vals.at[:, 0], both.at[p], c_sem.at[0], c_sem.at[1], core_id)
     tab_x.start()
     tab_c.start()
-    x_copy(sent_row(0)).start()
+    x_copy(sent_row(0), 0).start()
     core.start()
-    for h in range(1, band):
-        x_copy(sent_row(h)).start()
+    for h in range(1, band * PARTS):
+        x_copy(sent_row(h // PARTS), h % PARTS).start()
 
     acc[...] = jnp.zeros_like(acc)
     own.wait()
@@ -135,9 +143,6 @@
     @pl.when(has_to)
     def _():
         tab_f.start()
-
-    core.wait()
-    tab_c.wait()
 
     def a_row(i, carry):
         at = pl.ds(pl.multiple_of(i * 64, 64), 64)
@@ -156,8 +161,6 @@
             a_lo[t, at, :] = lo
         return carry
 
-    lax.fori_loop(0, band, a_row, 0)
-
     def spread(chunk, table, first, load):
         for r in range(CHUNK):
             stage[r] = load(chunk * CHUNK + r)
@@ -187,15 +190,16 @@
     everything = pl.ds(0, band * 64)
 
     def forward(h):
-        row = got_row(h)
-        x_copy(row).wait_recv()
+        row, part = got_row(h // PARTS), lax.rem(h, PARTS)
+        x_copy(row, part).wait_recv()
 
         @pl.when(has_to)
         def _():
-            f_copy(row).start()
+            f_copy(row, part).start()
 
     def from_relay(row):
-        f_copy(row).wait_recv()
+        for part in range(PARTS):
+            f_copy(row, part).wait_recv()
         return f_buf[row]
 
     def relay_chunk(m):
@@ -203,13 +207,23 @@
         return own_tile - x_shift + got_chunk(m)
 
     def step(m, carry):
-        forward(CHUNK * m)
+        h = CHUNK * PARTS * m
+
+        @pl.when(m == 0)
+        def _():
+            core.wait()
+            tab_c.wait()
+            lax.fori_loop(0, half, a_row, 0)
+
+        forward(h + 1)
+
+        @pl.when(m == 0)
+        def _():
+            lax.fori_loop(half, band, a_row, 0)
+
         spread(m, inv, OWN_AT, lambda row: both[p, row])
+        forward(h + 2)
         multiply(own_tile + m, everything)
-        for r in range(1, CHUNK):
-            forward(CHUNK * m + r)
-        spread(got_chunk(m), inv_x, X_AT, lambda row: x_buf[row])
-        multiply(own_tile + x_shift + got_chunk(m), everything)
 
         @pl.when(has_from & (m >= 1))
         def _():
@@ -219,8 +233,18 @@
 
             multiply(relay_chunk(m - 1), everything)
 
+        for later in range(3, CHUNK * PARTS):
+            forward(h + later)
+        spread(got_chunk(m), inv_x, X_AT, lambda row: x_buf[row])
+
+        @pl.when(m < chunks - 1)
+        def _():
+            forward(h + CHUNK * PARTS)
+
+        multiply(own_tile + x_shift + got_chunk(m), everything)
         return carry
 
+    forward(0)
     lax.fori_loop(0, chunks, step, 0)
 
     def out_row(i, carry):
@@ -233,12 +257,16 @@
         for t in range(slots // 2):
             put = 2 * t
             x = picked(pair(codes, put, codes, put + 1), held)
-            out[i, 0, :, t * 128:(t + 1) * 128] = x.reshape(64, 128)
+            out_v[i, :, t * 128:(t + 1) * 128] = x.reshape(64, 128)
         return carry
 
     last = got_chunk(chunks - 1) * CHUNK
     start = jnp.where(odd == 1, 0, CHUNK)
     lax.fori_loop(start, start + band - CHUNK, out_row, 0)
+    early, late = pl.ds(start, band - CHUNK), pl.ds(last, CHUNK)
+    write_early = pltpu.make_async_copy(out_v.at[early], out.at[early, 0], l_sem.at[2])
+    write_late = pltpu.make_async_copy(out_v.at[late], out.at[late, 0], l_sem.at[3])
+    write_early.start()
 
     @pl.when(has_from)
     def _():
@@ -246,15 +274,21 @@
         multiply(k_tile, pl.ds(pl.multiple_of(last * 64, 128), CHUNK * 64))
 
     lax.fori_loop(last, last + CHUNK, out_row, 0)
+    write_late.start()
 
     for row in range(band):
-        x_copy(row).wait_send()
+        for part in range(PARTS):
+            x_copy(row, part).wait_send()
 
     @pl.when(has_to)
     def _():
         tab_f.wait_send()
         for row in range(band):
-            f_copy(row).wait_send()
+            for part in range(PARTS):
+                f_copy(row, part).wait_send()
+
+    write_early.wait()
+    write_late.wait()
 
 
 def local(n_col, block_values, block_cols):
@@ -263,6 +297,7 @@
     rows = -(-band // 8) * 8
     k_tiles = (2 * REACH + band) // 2
     tiles = (k_tiles + 1) // 2
+    pieces = band * PARTS
     dma = pltpu.SemaphoreType.DMA
     return pl.pallas_call(
         functools.partial(kernel, n_col, band, slots),
@@ -271,9 +306,10 @@
             pl.BlockSpec(memory_space=pltpu.HBM),
             pl.BlockSpec(memory_space=pltpu.HBM),
         ],
-        out_specs=pl.BlockSpec(memory_space=pltpu.VMEM),
+        out_specs=pl.BlockSpec(memory_space=pltpu.HBM),
         scratch_shapes=[
             pltpu.VMEM((2, band, side, slots * side), jnp.float32),
+            pltpu.VMEM((band, side, slots * side), jnp.float32),
             pltpu.VMEM((band, side, slots * side), jnp.float32),
             pltpu.VMEM((band, side, slots * side), jnp.float32),
             pltpu.VMEM((CHUNK, side, slots * side), jnp.float32),
@@ -288,11 +324,11 @@
             pltpu.VMEM((rows, 128), jnp.int32),
             pltpu.VMEM((rows, 128), jnp.int32),
             pltpu.VMEM((rows, 128), jnp.int32),
-            dma((band,)), dma((band,)), dma((band,)), dma((band,)),
-            dma((2,)), dma((3,)), dma((3,)), dma((2,)),
+            dma((pieces,)), dma((pieces,)), dma((pieces,)), dma((pieces,)),
+            dma((2,)), dma((3,)), dma((3,)), dma((4,)),
         ],
         compiler_params=pltpu.CompilerParams(
-            collective_id=0, has_side_effects=True, vmem_limit_bytes=48 * 1024 * 1024
+            collective_id=0, has_side_effects=True, vmem_limit_bytes=60 * 1024 * 1024
         ),
     )(block_values, block_cols)
 

time: 52.1 us -> 49.7 us (0.954)
  Pallas kernels: 47.8 us -> 46.3 us
  local copies, waits for them, and re-layouts: 3.29 us -> 2.73 us
    pallas_call x1, Pallas kernels: 47.8 us -> 46.3 us  [local(): pl.pallas_call(functools.partial(kernel, n_col, band, slots), out_shape=j...]
    unnamed x5 -> x1, local copies, waits for them, and re-layouts: 3.29 us -> 2.73 us
where the time goes in v3:
time: 49.7 us; the launch traced here: 49 us
  Pallas kernels  46.3 us (93%)
  local copies, waits for them, and re-layouts  2.73 us (5%)
    pallas_call x1, Pallas kernels, local(): pl.pallas_call(functools.partial(kernel, n_col, band, slots), out_shape=j...  46.3 us
    unnamed x1, local copies, waits for them, and re-layouts  2.73 us

profile of v3, /device:TPU:8, one launch (start us, length us, event | category | flops | bytes accessed | tf_op | source)
XLA Modules:
  0.0 49.0 jit_solution(222351384199048754)
XLA Ops:
  0.0 46.3 %shard_map.28 = f32[10,1,64,640]{3,2,1,0:T(8,128)} custom-call(f32[10,1,64,640]{3,2,1,0:T(8,128)} %vals.1, s32[10,1,10]{2,1,0:T(1,128)} %cols.1), custom_call_target="tpu_custom_call" | custom-call | tf_op jit(solution)/shard_map/pallas_call | solution.py:302
  46.3 2.7 %copy.4 = f32[10,1,64,640]{3,2,1,0:T(8,128)} copy(f32[10,1,64,640]{3,2,1,0:T(8,128)} %shard_map.28) | data formatting | bytes 3276800

commit v4 on v3

--- a/solution.py
+++ b/solution.py
@@ -47,7 +47,7 @@
 
 def kernel(
     n_col, band, slots, vals, cols, out,
-    both, x_buf, f_buf, out_v, stage, b_hi, b_lo, a_hi, a_lo, acc, cols_v, put_v, inv, inv_o, inv_x, inv_f,
+    both, x_buf, f_buf, stage, b_hi, b_lo, a_hi, a_lo, acc, cols_v, put_v, inv, inv_o, inv_x, inv_f,
     x_send, x_recv, f_send, f_recv, c_sem, t_send, t_recv, l_sem,
 ):
     g, p, c = lax.axis_index("groups"), lax.axis_index("row"), lax.axis_index("col")
@@ -82,6 +82,42 @@
     def _():
         pl.semaphore_signal(barrier, inc=1, device_id=from_id, device_id_type=MESH)
 
+    pl.semaphore_wait(barrier, 2 + has_to.astype(jnp.int32) + has_from.astype(jnp.int32))
+
+    def remote(src, dst, send, recv, device):
+        return pltpu.make_async_remote_copy(
+            src_ref=src, dst_ref=dst, send_sem=send, recv_sem=recv,
+            device_id=device, device_id_type=MESH,
+        )
+
+    def x_copy(row, part):
+        at, sem = pl.ds(part * PIECE, PIECE), row * PARTS + part
+        return remote(
+            vals.at[row, 0, at], x_buf.at[row, at], x_send.at[sem], x_recv.at[sem], x_id
+        )
+
+    def f_copy(row, part):
+        at, sem = pl.ds(part * PIECE, PIECE), row * PARTS + part
+        return remote(
+            x_buf.at[row, at], f_buf.at[row, at], f_send.at[sem], f_recv.at[sem], to_id
+        )
+
+    def sent_row(h):
+        return jnp.where(odd == 1, band - 1 - h, h)
+
+    def got_row(h):
+        return jnp.where(odd == 1, h, band - 1 - h)
+
+    def got_chunk(m):
+        return jnp.where(odd == 1, m, chunks - 1 - m)
+
+    tab_c = remote(inv, inv_o, t_send.at[0], t_recv.at[0], core_id)
+    tab_x = remote(inv, inv_x, t_send.at[1], t_recv.at[1], x_id)
+    tab_f = remote(inv_x, inv_f, t_send.at[2], t_recv.at[2], to_id)
+    core = remote(vals.at[:, 0], both.at[p], c_sem.at[0], c_sem.at[1], core_id)
+    x_copy(sent_row(0), 0).start()
+    core.start()
+
     lists.wait()
     column = cols_v[:, 0, :]
     base = c * band - REACH + p
@@ -96,43 +132,8 @@
     inv[...] = jnp.full(inv.shape, -1, jnp.int32)
     inv[:band, :] = codes
     put_v[...] = jnp.where(column >= 0, (column - base) >> 1, -1)
-    pl.semaphore_wait(barrier, 2 + has_to.astype(jnp.int32) + has_from.astype(jnp.int32))
-
-    def remote(src, dst, send, recv, device):
-        return pltpu.make_async_remote_copy(
-            src_ref=src, dst_ref=dst, send_sem=send, recv_sem=recv,
-            device_id=device, device_id_type=MESH,
-        )
-
-    def x_copy(row, part):
-        at, sem = pl.ds(part * PIECE, PIECE), row * PARTS + part
-        return remote(
-            vals.at[row, 0, at], x_buf.at[row, at], x_send.at[sem], x_recv.at[sem], x_id
-        )
-
-    def f_copy(row, part):
-        at, sem = pl.ds(part * PIECE, PIECE), row * PARTS + part
-        return remote(
-            x_buf.at[row, at], f_buf.at[row, at], f_send.at[sem], f_recv.at[sem], to_id
-        )
-
-    def sent_row(h):
-        return jnp.where(odd == 1, band - 1 - h, h)
-
-    def got_row(h):
-        return jnp.where(odd == 1, h, band - 1 - h)
-
-    def got_chunk(m):
-        return jnp.where(odd == 1, m, chunks - 1 - m)
-
-    tab_c = remote(inv, inv_o, t_send.at[0], t_recv.at[0], core_id)
-    tab_x = remote(inv, inv_x, t_send.at[1], t_recv.at[1], x_id)
-    tab_f = remote(inv_x, inv_f, t_send.at[2], t_recv.at[2], to_id)
-    core = remote(vals.at[:, 0], both.at[p], c_sem.at[0], c_sem.at[1], core_id)
     tab_x.start()
     tab_c.start()
-    x_copy(sent_row(0), 0).start()
-    core.start()
     for h in range(1, band * PARTS):
         x_copy(sent_row(h // PARTS), h % PARTS).start()
 
@@ -163,8 +164,10 @@
 
     def spread(chunk, table, first, load):
         for r in range(CHUNK):
-            stage[r] = load(chunk * CHUNK + r)
-            codes = table[pl.ds(chunk * CHUNK + r, 1), :]
+            row = jnp.where(odd == 1, r, CHUNK - 1 - r)
+            at_row = pl.ds(pl.multiple_of(row * 64, 64), 64)
+            stage[r] = load(chunk * CHUNK + row)
+            codes = table[pl.ds(chunk * CHUNK + row, 1), :]
             held = []
             for u in range(slots // 2):
                 tile = stage[r, :, u * 128:(u + 1) * 128].reshape(8, 8, 128)
@@ -172,8 +175,8 @@
             for t in range(tiles):
                 at = first + 2 * t
                 hi, lo = split(picked(pair(codes, at, codes, at + 1), held))
-                b_hi[r * 64:(r + 1) * 64, t * 128:(t + 1) * 128] = hi
-                b_lo[r * 64:(r + 1) * 64, t * 128:(t + 1) * 128] = lo
+                b_hi[at_row, t * 128:(t + 1) * 128] = hi
+                b_lo[at_row, t * 128:(t + 1) * 128] = lo
 
     def multiply(k_tile, at):
         left_hi = a_hi[k_tile, at, :]
@@ -257,16 +260,12 @@
         for t in range(slots // 2):
             put = 2 * t
             x = picked(pair(codes, put, codes, put + 1), held)
-            out_v[i, :, t * 128:(t + 1) * 128] = x.reshape(64, 128)
+            out[i, 0, :, t * 128:(t + 1) * 128] = x.reshape(64, 128)
         return carry
 
     last = got_chunk(chunks - 1) * CHUNK
     start = jnp.where(odd == 1, 0, CHUNK)
     lax.fori_loop(start, start + band - CHUNK, out_row, 0)
-    early, late = pl.ds(start, band - CHUNK), pl.ds(last, CHUNK)
-    write_early = pltpu.make_async_copy(out_v.at[early], out.at[early, 0], l_sem.at[2])
-    write_late = pltpu.make_async_copy(out_v.at[late], out.at[late, 0], l_sem.at[3])
-    write_early.start()
 
     @pl.when(has_from)
     def _():
@@ -274,7 +273,6 @@
         multiply(k_tile, pl.ds(pl.multiple_of(last * 64, 128), CHUNK * 64))
 
     lax.fori_loop(last, last + CHUNK, out_row, 0)
-    write_late.start()
 
     for row in range(band):
         for part in range(PARTS):
@@ -286,9 +284,6 @@
         for row in range(band):
             for part in range(PARTS):
                 f_copy(row, part).wait_send()
-
-    write_early.wait()
-    write_late.wait()
 
 
 def local(n_col, block_values, block_cols):
@@ -306,10 +301,9 @@
             pl.BlockSpec(memory_space=pltpu.HBM),
             pl.BlockSpec(memory_space=pltpu.HBM),
         ],
-        out_specs=pl.BlockSpec(memory_space=pltpu.HBM),
+        out_specs=pl.BlockSpec(memory_space=pltpu.VMEM),
         scratch_shapes=[
             pltpu.VMEM((2, band, side, slots * side), jnp.float32),
-            pltpu.VMEM((band, side, slots * side), jnp.float32),
             pltpu.VMEM((band, side, slots * side), jnp.float32),
             pltpu.VMEM((band, side, slots * side), jnp.float32),
             pltpu.VMEM((CHUNK, side, slots * side), jnp.float32),
@@ -325,10 +319,10 @@
             pltpu.VMEM((rows, 128), jnp.int32),
             pltpu.VMEM((rows, 128), jnp.int32),
             dma((pieces,)), dma((pieces,)), dma((pieces,)), dma((pieces,)),
-            dma((2,)), dma((3,)), dma((3,)), dma((4,)),
+            dma((2,)), dma((3,)), dma((3,)), dma((2,)),
         ],
         compiler_params=pltpu.CompilerParams(
-            collective_id=0, has_side_effects=True, vmem_limit_bytes=60 * 1024 * 1024
+            collective_id=0, has_side_effects=True, vmem_limit_bytes=48 * 1024 * 1024
         ),
     )(block_values, block_cols)
 

time: 49.7 us -> 49.5 us (level)
  Pallas kernels: 46.3 us -> 45.7 us
  local copies, waits for them, and re-layouts: 2.73 us -> 3.29 us
    unnamed x1 -> x5, local copies, waits for them, and re-layouts: 2.73 us -> 3.29 us
    pallas_call x1, Pallas kernels: 46.3 us -> 45.7 us  [local(): pl.pallas_call(functools.partial(kernel, n_col, band, slots), out_shape=j...]
where the time goes in v4:
time: 49.5 us; the launch traced here: 49 us
  Pallas kernels  45.7 us (92%)
  local copies, waits for them, and re-layouts  3.29 us (7%)
    pallas_call x1, Pallas kernels, local(): pl.pallas_call(functools.partial(kernel, n_col, band, slots), out_shape=j...  45.7 us
    unnamed x5, local copies, waits for them, and re-layouts  3.29 us

profile of v4, /device:TPU:8, one launch (start us, length us, event | category | flops | bytes accessed | tf_op | source)
XLA Modules:
  0.0 49.0 jit_solution(4426398630834064297)
XLA Ops:
  0.0 0.0 copy-start
  0.0 1.4 %copy-done = f32[10,1,64,640]{3,2,1,0:T(8,128)S(1)} copy-done((f32[10,1,64,640]{3,2,1,0:T(8,128)S(1)}, f32[10,1,64,640]{3,2,1,0:T(8,128)}, u32[]{:S(2)}) %copy-start) | copy-done | bytes 1638424
  1.4 0.0 copy-start.1
  1.4 0.7 %copy-done.1 = s32[10,1,10]{2,1,0:T(1,128)S(1)} copy-done((s32[10,1,10]{2,1,0:T(1,128)S(1)}, s32[10,1,10]{2,1,0:T(1,128)}, u32[]{:S(2)}) %copy-start.1) | copy-done | bytes 424
  2.1 45.7 %shard_map.28 = f32[10,1,64,640]{3,2,1,0:T(8,128)S(1)} custom-call(f32[10,1,64,640]{3,2,1,0:T(8,128)S(1)} %copy-done, s32[10,1,10]{2,1,0:T(1,128)S(1)} %copy-done.1), custom_call_target="tpu_custom_call" | custom-call | tf_op jit(solution)/shard_map/pallas_call | solution.py:297
  47.9 1.2 %copy.4 = f32[10,1,64,640]{3,2,1,0:T(8,128)} copy(f32[10,1,64,640]{3,2,1,0:T(8,128)S(1)} %shard_map.28) | data formatting | bytes 3276800
Async XLA Ops:
  0.0 1.4 %copy-start = (f32[10,1,64,640]{3,2,1,0:T(8,128)S(1)}, f32[10,1,64,640]{3,2,1,0:T(8,128)}, u32[]{:S(2)}) copy-start(f32[10,1,64,640]{3,2,1,0:T(8,128)} %vals.1) | copy-start | bytes 4915204
  1.4 0.7 %copy-start.1 = (s32[10,1,10]{2,1,0:T(1,128)S(1)}, s32[10,1,10]{2,1,0:T(1,128)}, u32[]{:S(2)}) copy-start(s32[10,1,10]{2,1,0:T(1,128)} %cols.1) | copy-start | bytes 1204
